TPU v7x, 32 devices: a whole 2x2x4 slice. The times are simulated.
32 devices in a mesh: dp: 8 (over z, y), comp: 4 (over x, core).
Axes of the slice: x: 2, y: 2, z: 4, core: 2. Of those that a mesh axis runs over, the one named last changes fastest.
Arguments:
- points: bfloat16 [4096, 1024], P('dp'), may hold values from -6 to 6
- means: float32 [1024, 8192], P('dp', 'comp'), may hold values from -2.25 to 2.25
- variances: float32 [1024, 8192], P('dp', 'comp'), may hold values from 0.45 to 2.22
- log_weights: float32 [8192], P('comp'), may hold values from -4 to 4
- split_list: int32 [256, 2], replicated, may hold values from 0 to 8191, as said below
- prune_list: int32 [256], replicated, may hold values from 0 to 8191, as said below
Outputs:
- new_means: float32 [1024, 8192], P('dp', 'comp')
- new_variances: float32 [1024, 8192], P('dp', 'comp')
- new_log_weights: float32 [8192], P('comp')
Inputs may be any that keep to these rules, and one draw needn't show every extreme that they name: `split_list`: rows j * 64 to (j + 1) * 64 - 1 of column 0 name 64 distinct components among j * 2048 to (j + 1) * 2048 - 1; column 1 is a permutation of 0 to 255. `prune_list`: distinct components, none of them in column 0 of split_list, exactly 64 in each aligned block of 2048 ids.
All inputs are finite; a program needn't handle non-finite values.
Results may differ from a plain program's by a relative error of at most 0.004.
The roundings to bfloat16 on the way count: a program that leaves them out, or rounds other values in their place, can miss the bound.
Values may be sent and summed in bfloat16 or wider, within the bound.
A program may use at most 64 MiB of HBM per device.

v0:
```python
import math

import jax
import jax.numpy as jnp
from jax import lax
from jax.sharding import PartitionSpec as P

log_two_pi = math.log(2.0 * math.pi)
log_two = math.log(2.0)
prior_count = 1.0
split_scale = 0.5


def combined_all(value, axis, join):
    pieces = jax.tree.map(lambda part: lax.all_gather(part, axis), value)
    head = jax.tree.map(lambda part: part[0], pieces)
    tail = jax.tree.map(lambda part: part[1:], pieces)
    subtotal, _ = lax.scan(lambda subtotal, section: (join(subtotal, section), None), head, tail)
    return subtotal


def combine_parts(earlier, later):
    top = jnp.maximum(earlier[0], later[0])
    return (top, earlier[1] * jnp.exp(earlier[0] - top) + later[1] * jnp.exp(later[0] - top))


def per_device(points, means, variances, log_weights, split_list, prune_list):
    contract = (((0,), (0,)), ((), ()))
    k_dev = means.shape[1]
    d_slice = means.shape[0]
    features = points.shape[1]
    n_rows = points.shape[0]
    comp_index = lax.axis_index("comp")
    npts = n_rows * lax.axis_size("dp")
    n_components = k_dev * lax.axis_size("comp")
    precision = 1.0 / variances
    prec_low = precision.astype(jnp.bfloat16)
    pm_low = (precision * means).astype(jnp.bfloat16)
    partial_value = 0.5 * jnp.sum(jnp.log(precision), 0) - 0.5 * jnp.sum(
        precision * means * means, 0
    )
    const = log_weights + lax.psum(partial_value, "dp") - 0.5 * features * log_two_pi
    as_float = points.astype(jnp.float32)
    x_sq = (as_float * as_float).astype(jnp.bfloat16)
    start_scores = jnp.zeros((n_rows, k_dev), jnp.float32)
    sq_cols = x_sq
    pt_cols = points
    quad = jnp.dot(
        sq_cols,
        lax.all_gather(prec_low, "dp", axis=0, tiled=True),
        preferred_element_type=jnp.float32,
    )
    lin = jnp.dot(
        pt_cols,
        lax.all_gather(pm_low, "dp", axis=0, tiled=True),
        preferred_element_type=jnp.float32,
    )
    scores = start_scores - 0.5 * quad + lin
    scores = scores + const[None, :]
    local_max = jnp.max(scores, 1)
    local_sum = jnp.sum(jnp.exp(scores - local_max[:, None]), 1)
    row_top, row_sum = combined_all((local_max, local_sum), "comp", combine_parts)
    lse = row_top + jnp.log(row_sum)
    resp = jnp.exp(scores - lse[:, None]).astype(jnp.bfloat16)
    pt_cols = points
    sq_cols = x_sq
    first = lax.dot_general(pt_cols, resp, contract, preferred_element_type=jnp.float32)
    second = lax.dot_general(sq_cols, resp, contract, preferred_element_type=jnp.float32)
    moments = lax.psum_scatter(
        jnp.concatenate([first, second], axis=1).astype(jnp.bfloat16),
        "dp",
        scatter_dimension=0,
        tiled=True,
    ).astype(jnp.float32)
    sum_x = moments[:, :k_dev]
    sum_xx = moments[:, k_dev:]
    counts = lax.psum(jnp.sum(resp, 0, dtype=jnp.float32), "dp")
    total = counts + prior_count
    mean_new = (sum_x + prior_count * means) / total[None, :]
    var_new = (sum_xx + prior_count * (variances + means * means)) / total[
        None, :
    ] - mean_new * mean_new
    lw_new = jnp.log(total) - jnp.log(npts + n_components * prior_count)
    spl_dev = split_list.shape[0] // lax.axis_size("comp")
    own_sources = (
        lax.dynamic_slice_in_dim(split_list[:, 0], comp_index * spl_dev, spl_dev, 0)
        - comp_index * k_dev
    )
    columns = jnp.arange(k_dev, dtype=jnp.int32)
    source_hot = (own_sources[:, None] == columns[None, :]).astype(jnp.float32)
    src_mean = mean_new[:, own_sources]
    src_var = var_new[:, own_sources]
    src_weight = lw_new[own_sources]
    shift = split_scale * jnp.sqrt(src_var)
    got_mean, got_var, got_weight = (
        lax.all_gather(src_mean, "comp", axis=1, tiled=True),
        lax.all_gather(src_var, "comp", axis=1, tiled=True),
        lax.all_gather(src_weight, "comp", axis=0, tiled=True),
    )
    targets = prune_list[split_list[:, 1]] - comp_index * k_dev
    target_hot = (targets[:, None] == columns[None, :]).astype(jnp.float32)
    receives = jnp.sum(target_hot, 0) > 0.5
    stacked = jnp.concatenate(
        [got_mean - split_scale * jnp.sqrt(got_var), got_var, (got_weight - log_two)[None, :]],
        axis=0,
    )
    placed = jnp.dot(stacked, target_hot, precision=lax.Precision.HIGHEST)
    moved_mean = mean_new + jnp.dot(shift, source_hot, precision=lax.Precision.HIGHEST)
    new_means = jnp.where(receives[None, :], placed[:d_slice], moved_mean)
    new_variances = jnp.where(receives[None, :], placed[d_slice : 2 * d_slice], var_new)
    lowered = lw_new - log_two * jnp.sum(source_hot, 0)
    new_log_weights = jnp.where(receives, placed[2 * d_slice], lowered)
    return (new_means, new_variances, new_log_weights)


def solution(mesh):
    in_specs = (P("dp", None), P("dp", "comp"), P("dp", "comp"), P("comp"), P(), P())
    out_specs = (P("dp", "comp"), P("dp", "comp"), P("comp"))
    return jax.shard_map(
        per_device, mesh=mesh, in_specs=in_specs, out_specs=out_specs, check_vma=False
    )
```

profile of v0, /device:TPU:13, one launch (start us, length us, event | category | flops | bytes accessed | tf_op | source)
XLA Modules:
  0.0 384.9 jit_solution(3657776960487092316)
XLA Ops:
  7.2 2.9 log_reduce_fusion
  11.0 12.2 %psum.14 = f32[2048]{0:T(1024)S(1)} all-reduce(f32[2048]{0:T(1024)S(1)} %multiply_subtract_fusion.1), channel_id=1, replica_groups=mesh['dp'=8,'comp'=4] {'dp'}, use_global_device_ids=true, to_apply=%region_3.0 | all-reduce | flops 2048 | bytes 16384 | tf_op jit(solution)/shard_map/psum | solution.py:42
  23.3 59.7 %all-gather.10.cloned.1.call-done = bf16[1024,2048]{1,0:T(8,128)(2,1)} async-done(((bf16[128,2048]{1,0:T(8,128)(2,1)}), bf16[1024,2048]{1,0:T(8,128)(2,1)}) %all-gather.10.cloned.1.call-update) | async-done | bytes 4194320 | tf_op jit(solution)/shard_map/all_gather | solution.py:50
  83.0 6.5 %fusion.7 = f32[512,2048]{1,0:T(8,128)} fusion(bf16[1024,2048]{1,0:T(8,128)(2,1)} %all-gather.10.cloned.1.call-done, bf16[512,1024]{1,0:T(8,128)(2,1)S(1)} %copy-done.5), kind=kOutput, calls=%fused_computation.31 | convolution fusion | flops 2149056512 | bytes 9437184 | tf_op jit(solution)/shard_map/dot_general | solution.py:48
  89.5 67.9 %all-gather.12.cloned.1.call-done = bf16[1024,2048]{1,0:T(8,128)(2,1)} async-done(((bf16[128,2048]{1,0:T(8,128)(2,1)}), bf16[1024,2048]{1,0:T(8,128)(2,1)}) %all-gather.12.cloned.1.call-update) | async-done | bytes 4194320 | tf_op jit(solution)/shard_map/all_gather | solution.py:55
  157.3 6.1 %fusion.25 = (f32[512]{0:T(512)S(1)}, f32[512,2048]{1,0:T(8,128)S(1)}) fusion(f32[2048]{0:T(1024)S(1)} %add_add_fusion, bf16[512,1024]{1,0:T(8,128)(2,1)S(1)} %copy-done.5, bf16[1024,2048]{1,0:T(8,128)(2,1)} %all-gather.12.cloned.1.call-done, f32[512,2048]{1,0:T(8,128)} %fusion.7), kind=kOutput, calls=%fused_computation.68 | convolution fusion | flops 2152726016 | bytes 13641728 | tf_op jit(solution)/shard_map/dot_general | solution.py:53
  163.5 1.9 copy-done.1
  166.1 6.7 %all-gather.6 = f32[4,1,512]{2,1,0:T(1,128)S(1)} all-gather(f32[1,1,512]{2,1,0:T(1,128)S(1)} %bitcast.53), channel_id=3, replica_groups=mesh['dp'=8,'comp'=4] {'comp'}, dimensions={0}, use_global_device_ids=true | all-gather | bytes 10240 | tf_op jit(solution)/shard_map/all_gather | solution.py:15
  172.8 5.3 %all-gather.5 = f32[4,1,512]{2,1,0:T(1,128)S(1)} all-gather(f32[1,1,512]{2,1,0:T(1,128)S(1)} %bitcast.52), channel_id=2, replica_groups=mesh['dp'=8,'comp'=4] {'comp'}, dimensions={0}, use_global_device_ids=true | all-gather | bytes 10240 | tf_op jit(solution)/shard_map/all_gather | solution.py:15
  178.3 2.9 convert_reduce_fusion
  181.2 4.4 %convert_bitcast_fusion = bf16[1024,2048]{0,1:T(8,128)(2,1)} fusion(bf16[512,2048]{1,0:T(8,128)(2,1)S(1)} %get-tuple-element.58, bf16[512,1024]{1,0:T(8,128)(2,1)S(1)} %copy-done.5), kind=kOutput, calls=%fused_computation.11 | convolution fusion | flops 2149580800 | bytes 7340032 | tf_op jit(solution)/shard_map/dot_general | solution.py:67
  185.5 4.4 %convolution_convert_fusion = bf16[1024,2048]{0,1:T(8,128)(2,1)} fusion(bf16[512,2048]{1,0:T(8,128)(2,1)S(1)} %get-tuple-element.58, bf16[512,1024]{1,0:T(8,128)(2,1)S(1)} %copy-done.5), kind=kOutput, calls=%fused_computation.14 | convolution fusion | flops 2151153664 | bytes 7340032 | tf_op jit(solution)/shard_map/dot_general | solution.py:68
  189.9 7.7 %pad_maximum_fusion = bf16[1024,4096]{0,1:T(8,128)(2,1)} fusion(bf16[1024,2048]{0,1:T(8,128)(2,1)} %convolution_convert_fusion, bf16[1024,2048]{0,1:T(8,128)(2,1)} %convert_bitcast_fusion), kind=kLoop, calls=%fused_computation.7 | loop fusion | flops 16777216 | bytes 16777216 | tf_op jit(solution)/shard_map/concatenate | solution.py:70
  197.6 11.5 %copy.46 = bf16[1024,4096]{1,0:T(8,128)(2,1)} copy(bf16[1024,4096]{0,1:T(8,128)(2,1)} %pad_maximum_fusion) | data formatting | bytes 16777216
  211.0 1.9 gather_fusion
  213.5 14.9 %psum.15 = f32[2048]{0:T(1024)S(1)} all-reduce(f32[2048]{0:T(1024)S(1)} %get-tuple-element.57), channel_id=1, replica_groups=mesh['dp'=8,'comp'=4] {'dp'}, use_global_device_ids=true, to_apply=%region_10.11 | all-reduce | flops 2048 | bytes 16384 | tf_op jit(solution)/shard_map/psum | solution.py:77
  229.5 7.4 %all-reduce = f32[256]{0:T(256)S(1)} all-reduce(f32[256]{0:T(256)S(1)} %dynamic-update-slice), channel_id=6, replica_groups=mesh['dp'=8,'comp'=4] {'comp'}, use_global_device_ids=true, to_apply=%add | all-reduce | flops 256 | bytes 2048
  237.0 120.2 %reduce-scatter.4.cloned.1.call-done = bf16[128,4096]{1,0:T(8,128)(2,1)} async-done(((bf16[1024,4096]{1,0:T(8,128)(2,1)}), bf16[128,4096]{1,0:T(8,128)(2,1)}) %reduce-scatter.4.cloned.1.call-update) | async-done | bytes 1048592 | tf_op jit(solution)/shard_map/reduce_scatter | solution.py:69
  357.2 1.4 convert_element_type.34
  358.6 1.6 fusion.4
  361.2 6.1 %all-gather.2 = f32[128,256]{0,1:T(8,128)S(1)} all-gather(f32[128,64]{0,1:T(8,128)S(1)} %bitcast.44), channel_id=4, replica_groups=mesh['dp'=8,'comp'=4] {'comp'}, dimensions={1}, use_global_device_ids=true | all-gather | bytes 163840 | tf_op jit(solution)/shard_map/all_gather | solution.py:96
  368.2 5.4 %all-gather.3 = f32[128,256]{0,1:T(8,128)S(1)} all-gather(f32[128,64]{0,1:T(8,128)S(1)} %bitcast.43), channel_id=5, replica_groups=mesh['dp'=8,'comp'=4] {'comp'}, dimensions={1}, use_global_device_ids=true | all-gather | bytes 163840 | tf_op jit(solution)/shard_map/all_gather | solution.py:97
  373.7 1.3 fusion.2
  376.7 1.7 fusion.1
  (58 shorter events, 8.4 us)
Async XLA Ops:
  7.2 203.8 %copy-start = (s32[256]{0:T(256)S(1)}, s32[256]{0:T(256)}, u32[]{:S(2)}) copy-start(s32[256]{0:T(256)} %param.13) | copy-start | bytes 3076
  7.2 16.1 %copy-start.3 = (f32[2048]{0:T(1024)S(1)}, f32[2048]{0:T(1024)}, u32[]{:S(2)}) copy-start(f32[2048]{0:T(1024)} %param.11) | copy-start | bytes 24580
  7.2 75.8 %copy-start.5 = (bf16[512,1024]{1,0:T(8,128)(2,1)S(1)}, bf16[512,1024]{1,0:T(8,128)(2,1)}, u32[]{:S(2)}) copy-start(bf16[512,1024]{1,0:T(8,128)(2,1)} %param.8) | copy-start | bytes 3145732
  7.2 75.7 %all-gather.10.cloned.1.call-start = ((), (), s32[]{:S(2)}) async-start(), calls=%async_computation.1 | async-start | bytes 4718592 | tf_op jit(solution)/shard_map/all_gather | solution.py:50
  10.2 147.1 %all-gather.12.cloned.1.call-start = ((), (), s32[]{:S(2)}) async-start(), calls=%async_computation.2 | async-start | bytes 4718592 | tf_op jit(solution)/shard_map/all_gather | solution.py:55
  11.0 346.2 %reduce-scatter.4.cloned.1.call-start = ((), (), s32[]{:S(2)}) async-start(), calls=%async_computation.3 | async-start | bytes 9437184 | tf_op jit(solution)/shard_map/reduce_scatter | solution.py:69
  163.4 1.9 copy-start.1
  209.1 0.7 copy-start.6
  209.1 1.9 copy-start.4
  209.1 149.5 %copy-start.2 = (f32[128,2048]{1,0:T(8,128)S(1)}, f32[128,2048]{1,0:T(8,128)}, u32[]{:S(2)}) copy-start(f32[128,2048]{1,0:T(8,128)} %param.10) | copy-start | bytes 3145732
Sparse Core Ops, SparseCore 0:
  10.7 72.1 all-gather.9
  85.6 71.6 all-gather.11
  209.2 147.9 reduce-scatter.3
where the time goes:
time: 388 us; the launch traced here: 385 us
  waiting for transfers between devices  248 us (64%)
  blocking collectives  58 us (15%)
  matrix products  24.3 us (6%)
  other arithmetic  19.7 us (5%)
  local copies, waits for them, and re-layouts  19.6 us (5%)
  between operations  14.7 us (4%)
    reduce_scatter x1, waiting for transfers between devices, per_device(): lax.psum_scatter(jnp.concatenate([first, second], axis=1).astype(jnp.bflo...  120 us
    all_gather x1, waiting for transfers between devices, per_device(): lax.all_gather(pm_low, 'dp', axis=0, tiled=True)  67.9 us
    all_gather x1, waiting for transfers between devices, per_device(): lax.all_gather(prec_low, 'dp', axis=0, tiled=True)  59.7 us
    psum x1, blocking collectives, per_device(): counts = lax.psum(jnp.sum(resp, 0, dtype=jnp.float32), 'dp')  14.9 us
    unnamed x20, local copies, waits for them, and re-layouts  14.9 us
    psum x1, blocking collectives, per_device(): lax.psum(partial_value, 'dp')  12.2 us
    all_gather x2, blocking collectives, combined_all(): pieces = jax.tree.map(lambda part: lax.all_gather(part, axis), value)  12 us
  transfers between devices with their start and end apart: 3, of which 3 were waited for; matrix products, arithmetic and copies ran while one was open for 3% of the time, Pallas kernels for 0%

commit v1 on v0

v1 whole, which is shorter than its diff:
```python
import functools
import math

import jax
import jax.numpy as jnp
from jax import lax
from jax.experimental import pallas as pl
from jax.experimental.pallas import tpu as pltpu
from jax.sharding import PartitionSpec as P

log_two_pi = math.log(2.0 * math.pi)
log_two = math.log(2.0)
prior_count = 1.0
split_scale = 0.5
MESH = pl.DeviceIdType.MESH
BF = jnp.bfloat16
F32 = jnp.float32
NT = (((1,), (1,)), ((), ()))


def aligned(index, step):
    return pl.ds(pl.multiple_of(index * step, step), step)


def kernel(
    n_dp, n_comp,
    pts, means, variances, weights, split, prune,
    out_mean, out_var, out_weight,
    allp, prm, par, par_t, cst_s, cst_r, scores, part_c, part_d, lse, resp,
    mom_s, mom_r, cnt_s, cnt_r, new_m, new_v, new_w, pay, got,
    z_s, z_r, y_s, y_r, x_s, x_r, c_s, c_r, p_s, p_r, k_s, k_r,
    lc_s, lc_r, ld_s, ld_r, m_s, m_r, n_s, n_r, g_s, g_r,
):
    rows, feats = pts.shape
    width, k_dev = means.shape
    chunk = k_dev // n_dp
    piece = rows // n_comp
    spl = split.shape[0] // n_comp
    far = 4 if n_dp % 4 == 0 else 1
    near = n_dp // far
    pairs = n_comp // 2
    i = lax.axis_index("dp")
    j = lax.axis_index("comp")
    a, b = i // near, i % near
    pair, core = j // 2, j % 2

    barrier = pltpu.get_barrier_semaphore()
    for r in range(1, n_dp):
        pl.semaphore_signal(barrier, inc=1, device_id=((i + r) % n_dp, j), device_id_type=MESH)
    for r in range(1, n_comp):
        pl.semaphore_signal(barrier, inc=1, device_id=(i, (j + r) % n_comp), device_id_type=MESH)
    pl.semaphore_wait(barrier, n_dp + n_comp - 2)

    def remote(src, dst, send, recv, to_i, to_j):
        return pltpu.make_async_remote_copy(
            src_ref=src, dst_ref=dst, send_sem=send, recv_sem=recv,
            device_id=(to_i, to_j), device_id_type=MESH,
        )

    def block_of(s, t):
        return ((a + far - s) % far) * near + (b + near - t) % near

    def place(block, quarter):
        return allp.at[aligned(block * n_comp + quarter, piece), :]

    def own_piece():
        return pts.at[aligned(j, piece), :]

    def z_copy(s):
        return remote(own_piece(), place(i, j), z_s.at[s], z_r.at[s], ((a + s) % far) * near + b, j)

    def y_copy(s, t):
        src = place(block_of(s, 0), j)
        return remote(src, src, y_s.at[s, t], y_r.at[s, t], a * near + (b + t) % near, j)

    def x_copy(idx, u):
        src = place(block_of(idx // near, idx % near), j)
        return remote(src, src, x_s.at[idx, u], x_r.at[idx, u], i, ((pair + u) % pairs) * 2 + core)

    def c_copy(idx, u):
        quarter = ((pair + pairs - u) % pairs) * 2 + core
        src = place(block_of(idx // near, idx % near), quarter)
        return remote(src, src, c_s.at[idx, u], c_r.at[idx, u], i, pair * 2 + 1 - core)

    for s in range(1, far):
        z_copy(s).start()
    allp[aligned(i, rows), :] = pts[...]
    for t in range(1, near):
        y_copy(0, t).start()

    def make_params(to):
        cols = aligned(to, chunk)
        v = variances[:, cols]
        m = means[:, cols]
        p = 1.0 / v
        pm = p * m
        prm[0, :, cols] = p.astype(BF)
        prm[1, :, cols] = pm.astype(BF)
        part = -0.5 * jnp.sum(jnp.log(v) + pm * m, 0, keepdims=True)
        cst_s[:, cols] = jnp.broadcast_to(part, (8, chunk))

    def p_copy(r):
        to = (i + r) % n_dp
        return remote(prm.at[:, :, aligned(to, chunk)], par.at[:, aligned(i, width), :], p_s.at[r], p_r.at[r], to, j)

    def k_copy(r):
        to = (i + r) % n_dp
        return remote(cst_s.at[:, aligned(to, chunk)], cst_r.at[i], k_s.at[r], k_r.at[r], to, j)

    def send_params(r, carry):
        make_params((i + r) % n_dp)
        p_copy(r).start()
        k_copy(r).start()
        return carry

    lax.fori_loop(1, n_dp, send_params, 0)
    make_params(i)
    par[:, aligned(i, width), :] = prm[:, :, aligned(i, chunk)]
    cst_r[i] = cst_s[:, aligned(i, chunk)]

    def pass_on(idx):
        for u in range(1, pairs):
            x_copy(idx, u).start()
        c_copy(idx, 0).start()

    for s in range(1, far):
        z_copy(s).wait_recv()
        for t in range(1, near):
            y_copy(s, t).start()
        pass_on(s * near)
    for s in range(far):
        for t in range(1, near):
            y_copy(s, t).wait_recv()
            pass_on(s * near + t)

    def wait_params(r, carry):
        p_copy(r).wait_recv()
        k_copy(r).wait_recv()
        return carry

    lax.fori_loop(1, n_dp, wait_params, 0)
    par_t[0] = (-0.5 * par[0].astype(F32)).T.astype(BF)
    par_t[1] = par[1].astype(F32).T.astype(BF)
    const_row = jnp.sum(cst_r[...], 0) + weights[:, aligned(i, chunk)] - 0.5 * feats * log_two_pi
    const = const_row.T[:, :1]

    def score(block):
        x = allp[aligned(block, rows), :]
        s = (
            lax.dot_general(par_t[0], x * x, NT, preferred_element_type=F32)
            + lax.dot_general(par_t[1], x, NT, preferred_element_type=F32)
            + const
        )
        scores[block] = s
        top = jnp.max(s, 0, keepdims=True)
        part_c[j, pl.ds(block, 1), :] = top + jnp.log(jnp.sum(jnp.exp(s - top), 0, keepdims=True))

    score(i)

    def score_step(idx, carry):
        for u in range(1, pairs):
            x_copy(idx, u).wait_recv()
            c_copy(idx, u).start()
        for u in range(pairs):
            c_copy(idx, u).wait_recv()
        score(block_of(idx // near, idx % near))
        return carry

    lax.fori_loop(1, n_dp, score_step, 0)

    def joined(parts):
        top = jnp.max(parts, 0)
        return top + jnp.log(jnp.sum(jnp.exp(parts - top[None]), 0))

    def lc_copy(r):
        return remote(part_c.at[j], part_c.at[j], lc_s.at[r], lc_r.at[r], i, (j + r) % n_comp)

    def ld_copy(r):
        return remote(part_d.at[i], part_d.at[i], ld_s.at[r], ld_r.at[r], (i + r) % n_dp, j)

    for r in range(1, n_comp):
        lc_copy(r).start()
    for r in range(1, n_comp):
        lc_copy(r).wait_recv()
    part_d[i] = joined(part_c[...])
    for r in range(1, n_dp):
        ld_copy(r).start()
    for r in range(1, n_dp):
        ld_copy(r).wait_recv()
    lse[...] = joined(part_d[...])

    def respond(block, carry):
        value = jnp.exp(scores[block] - lse[pl.ds(block, 1), :]).astype(BF)
        resp[:, aligned(block, rows)] = value
        return carry + lax.dot_general(jnp.ones((8, rows), BF), value, NT, preferred_element_type=F32)

    cnt_s[...] = lax.fori_loop(0, n_dp, respond, jnp.zeros((8, chunk), F32))

    def n_copy(r):
        return remote(cnt_s, cnt_r.at[:, aligned(i, chunk)], n_s.at[r], n_r.at[r], (i + r) % n_dp, j)

    for r in range(1, n_dp):
        n_copy(r).start()
    cnt_r[:, aligned(i, chunk)] = cnt_s[...]

    def m_copy(r):
        to = (i + r) % n_dp
        return remote(
            mom_s.at[:, aligned(to, width), :], mom_r.at[:, :, aligned(i, chunk)], m_s.at[r], m_r.at[r], to, j
        )

    wide = max(width, 256)
    each = wide // width
    groups = feats // wide
    mine = i // each

    def moment(group):
        cols = aligned(group, wide)
        x = allp[:, cols]
        mom_s[0, cols, :] = jnp.dot(resp[...], x, preferred_element_type=F32).T.astype(BF)
        mom_s[1, cols, :] = jnp.dot(resp[...], x * x, preferred_element_type=F32).T.astype(BF)

    def moment_step(g, carry):
        group = (mine + g) % groups
        moment(group)
        for e in range(each):
            m_copy((group * each + e + n_dp - i) % n_dp).start()
        return carry

    lax.fori_loop(1, groups, moment_step, 0)
    moment(mine)
    for e in range(1, each):
        to = mine * each + (i % each + e) % each
        m_copy((to + n_dp - i) % n_dp).start()
    mom_r[:, :, aligned(i, chunk)] = mom_s[:, aligned(i, width), :]

    base = (j * k_dev).astype(F32)
    sources = split[aligned(j, spl), :][:, 0:1].astype(F32) - base
    n_total = math.log(n_dp * rows + n_comp * k_dev * prior_count)
    pay[...] = jnp.zeros_like(pay)

    def hot(ids, at):
        ids_at = lax.broadcasted_iota(jnp.int32, (ids.shape[0], chunk), 1) + at * chunk
        return ids == ids_at.astype(F32)

    def finish(at):
        cols = aligned(at, chunk)
        total = cnt_r[0:1, cols] + prior_count
        inverse = 1.0 / total
        old = means[:, cols]
        mean = (mom_r[0, :, cols].astype(F32) + prior_count * old) * inverse
        var = (mom_r[1, :, cols].astype(F32) + prior_count * (variances[:, cols] + old * old)) * inverse - mean * mean
        low = jnp.log(total) - n_total
        here = hot(sources, at)
        here_f = jnp.where(here, 1.0, 0.0)
        source = jnp.max(here_f, 0, keepdims=True)
        shift = jnp.where(source > 0.5, split_scale * jnp.sqrt(var), 0.0)
        low = low - log_two * source
        new_m[:, cols] = mean + shift
        new_v[:, cols] = var
        new_w[:, cols] = low
        low_high = low.astype(BF)
        low_rest = (low - low_high.astype(F32)).astype(BF)
        here_b = here_f.astype(BF)
        pay[0, :width, :] += lax.dot_general((mean - shift).astype(BF), here_b, NT, preferred_element_type=F32)
        pay[1, :width, :] += lax.dot_general(var.astype(BF), here_b, NT, preferred_element_type=F32)
        spread = lambda row: jnp.broadcast_to(row, (8, chunk))
        pay[0, width:, :] += lax.dot_general(spread(low_high), here_b, NT, preferred_element_type=F32)
        pay[1, width:, :] += lax.dot_general(spread(low_rest), here_b, NT, preferred_element_type=F32)

    finish(i)

    def finish_step(r, carry):
        n_copy(r).wait_recv()
        m_copy(r).wait_recv()
        finish((i + n_dp - r) % n_dp)
        return carry

    lax.fori_loop(1, n_dp, finish_step, 0)

    extra = 16
    got[j, :width, :] = jnp.concatenate([pay[0, :width, :], pay[1, :width, :]], 1).astype(BF)
    got[j, width : width + extra, :] = jnp.concatenate(
        [
            jnp.concatenate([pay[0, width:, :], pay[1, width:, :]], 1),
            jnp.ones((8, 2 * spl), F32),
        ],
        0,
    ).astype(BF)

    def g_copy(r):
        return remote(got.at[j], got.at[j], g_s.at[r], g_r.at[r], i, (j + r) % n_comp)

    for r in range(1, n_comp):
        g_copy(r).start()
    slots = split[:, 1:2]
    slot_at = lax.broadcasted_iota(jnp.int32, (split.shape[0], split.shape[0]), 1)
    targets = jnp.sum(jnp.where(slots == slot_at, prune[...].astype(F32), 0.0), 1, keepdims=True) - base
    blank = jnp.full((spl, 1), -1.0, F32)
    parts = [targets[q * spl : (q + 1) * spl] for q in range(n_comp)]
    left = jnp.concatenate([part for q in range(n_comp) for part in (parts[q], blank)], 0)
    right = jnp.concatenate([part for q in range(n_comp) for part in (blank, parts[q])], 0)
    for r in range(1, n_comp):
        g_copy(r).wait_recv()
    cat = jnp.concatenate([got[q] for q in range(n_comp)], 1)

    for at in range(n_dp):
        cols = pl.ds(at * chunk, chunk)
        hot_l = jnp.where(hot(left, at), 1.0, 0.0).astype(BF)
        hot_r = jnp.where(hot(right, at), 1.0, 0.0).astype(BF)
        got_m = jnp.dot(cat, hot_l, preferred_element_type=F32)
        got_v = jnp.dot(cat, hot_r, preferred_element_type=F32)
        takes = got_m[width + 8 : width + 9, :] > 0.5
        out_mean[:, cols] = jnp.where(takes, got_m[:width], new_m[:, cols])
        out_var[:, cols] = jnp.where(takes, got_v[:width], new_v[:, cols])
        moved = got_m[width : width + 1, :] + got_v[width : width + 1, :]
        out_weight[:, cols] = jnp.where(takes, moved, new_w[:, cols])

    for s in range(1, far):
        z_copy(s).wait_send()
    for s in range(far):
        for t in range(1, near):
            y_copy(s, t).wait_send()

    def drain(idx, carry):
        for u in range(1, pairs):
            x_copy(idx, u).wait_send()
        for u in range(pairs):
            c_copy(idx, u).wait_send()
        p_copy(idx).wait_send()
        k_copy(idx).wait_send()
        ld_copy(idx).wait_send()
        n_copy(idx).wait_send()
        m_copy(idx).wait_send()
        return carry

    lax.fori_loop(1, n_dp, drain, 0)
    for r in range(1, n_comp):
        lc_copy(r).wait_send()
        g_copy(r).wait_send()


def solution(mesh):
    n_dp, n_comp = mesh.shape["dp"], mesh.shape["comp"]

    def per_device(points, means, variances, log_weights, split_list, prune_list):
        rows, feats = points.shape
        width, k_dev = means.shape
        chunk = k_dev // n_dp
        npts = rows * n_dp
        spl = split_list.shape[0] // n_comp
        far = 4 if n_dp % 4 == 0 else 1
        near, pairs = n_dp // far, n_comp // 2
        sem = lambda *shape: [pltpu.SemaphoreType.DMA(shape), pltpu.SemaphoreType.DMA(shape)]
        vmem = pl.BlockSpec(memory_space=pltpu.VMEM)
        out = pl.pallas_call(
            functools.partial(kernel, n_dp, n_comp),
            out_shape=(
                jax.ShapeDtypeStruct((width, k_dev), F32),
                jax.ShapeDtypeStruct((width, k_dev), F32),
                jax.ShapeDtypeStruct((1, k_dev), F32),
            ),
            in_specs=[vmem] * 6,
            out_specs=(vmem, vmem, vmem),
            scratch_shapes=[
                pltpu.VMEM((npts, feats), BF),
                pltpu.VMEM((2, width, k_dev), BF),
                pltpu.VMEM((2, feats, chunk), BF),
                pltpu.VMEM((2, chunk, feats), BF),
                pltpu.VMEM((8, k_dev), F32),
                pltpu.VMEM((n_dp, 8, chunk), F32),
                pltpu.VMEM((n_dp, chunk, rows), F32),
                pltpu.VMEM((n_comp, n_dp, rows), F32),
                pltpu.VMEM((n_dp, n_dp, rows), F32),
                pltpu.VMEM((n_dp, rows), F32),
                pltpu.VMEM((chunk, npts), BF),
                pltpu.VMEM((2, feats, chunk), BF),
                pltpu.VMEM((2, width, k_dev), BF),
                pltpu.VMEM((8, chunk), F32),
                pltpu.VMEM((8, k_dev), F32),
                pltpu.VMEM((width, k_dev), F32),
                pltpu.VMEM((width, k_dev), F32),
                pltpu.VMEM((1, k_dev), F32),
                pltpu.VMEM((2, width + 8, spl), F32),
                pltpu.VMEM((n_comp, width + 16, 2 * spl), BF),
                *sem(far), *sem(far, near), *sem(n_dp, pairs), *sem(n_dp, pairs),
                *sem(n_dp), *sem(n_dp), *sem(n_comp), *sem(n_dp), *sem(n_dp), *sem(n_dp), *sem(n_comp),
            ],
            compiler_params=pltpu.CompilerParams(
                collective_id=0, has_side_effects=True, vmem_limit_bytes=56 * 1024 * 1024
            ),
        )(points, means, variances, log_weights[None, :], split_list, prune_list[None, :])
        return out[0], out[1], out[2][0]

    in_specs = (P("dp", None), P("dp", "comp"), P("dp", "comp"), P("comp"), P(), P())
    out_specs = (P("dp", "comp"), P("dp", "comp"), P("comp"))
    return jax.shard_map(per_device, mesh=mesh, in_specs=in_specs, out_specs=out_specs, check_vma=False)
```

time: 388 us -> 121 us (0.31)
  waiting for transfers between devices: 248 us -> 0 us
  Pallas kernels: 0 us -> 115 us
  blocking collectives: 58 us -> 0 us
  matrix products: 24.3 us -> 0 us
  other arithmetic: 19.7 us -> 0 us
  local copies, waits for them, and re-layouts: 19.6 us -> 5.43 us
  between operations: 14.7 us -> 0.66 us
    all_gather x2 -> x0, waiting for transfers between devices: 128 us -> none  [the longest x1 67.9 us: per_device(): lax.all_gather(pm_low, 'dp', axis=0, tiled=True)]
    reduce_scatter x1 -> x0, waiting for transfers between devices: 120 us -> none  [per_device(): lax.psum_scatter(jnp.concatenate([first, second], axis=1).astype(jnp.bflo...]
    pallas_call x0 -> x1, Pallas kernels: none -> 115 us  [per_device(): pl.pallas_call(functools.partial(kernel, n_dp, n_comp), out_shape=(jax.Sh...]
    psum x2 -> x0, blocking collectives: 27.1 us -> none  [the longest x1 14.9 us: per_device(): counts = lax.psum(jnp.sum(resp, 0, dtype=jnp.float32), 'dp')]
    dot_general x6 -> x0, matrix products: 24.3 us -> none  [the longest x1 6.5 us: per_device(): jnp.dot(sq_cols, lax.all_gather(prec_low, 'dp', axis=0, tiled=True), pref...]
    all_gather x4 -> x0, blocking collectives: 23.5 us -> none  [the longest x2 12 us: combined_all(): pieces = jax.tree.map(lambda part: lax.all_gather(part, axis), value)]
    unnamed x20 -> x10, local copies, waits for them, and re-layouts: 14.9 us -> 5.43 us
    concatenate x1 -> x0, other arithmetic: 7.67 us -> none  [per_device(): jnp.concatenate([first, second], axis=1).astype(jnp.bfloat16)]
  transfers between devices with their start and end apart: 3 -> 0, of which waited for: 3 -> 0; matrix products, arithmetic and copies ran while one was open for 3% -> 0% of each run, Pallas kernels for 0% -> 0%
where the time goes in v1:
time: 121 us
  Pallas kernels  115 us (95%)
  local copies, waits for them, and re-layouts  5.43 us (4%)
    pallas_call x1, Pallas kernels, per_device(): pl.pallas_call(functools.partial(kernel, n_dp, n_comp), out_shape=(jax.Sh...  115 us
    unnamed x10, local copies, waits for them, and re-layouts  5.43 us

profile of v1, /device:TPU:13, one launch (start us, length us, event | category | flops | bytes accessed | tf_op | source)
XLA Modules:
  0.0 121.3 jit_solution(7988416137327078495)
XLA Ops:
  0.6 0.0 copy-start.2
  0.6 0.7 copy-done.2
  1.3 0.8 copy.9.split
  2.1 115.2 %shard_map.85 = (f32[128,2048]{1,0:T(8,128)}, f32[128,2048]{1,0:T(8,128)}, f32[1,2048]{1,0:T(1,128)}) custom-call(bf16[512,1024]{1,0:T(8,128)(2,1)} %pts.1, f32[128,2048]{1,0:T(8,128)} %means.1, f32[128,2048]{1,0:T(8,128)} %variances.1, f32[1,2048]{1,0:T(1,128)} %bitcast.3, s32[256,2]{1,0:T(8,128)} %copy.9.split, s32[1,256]{1,0:T(1,128)} %bitcast.5), custom_call_target="tpu_custom_call" | custom-call | tf_op jit(solution)/shard_map/pallas_call | solution.py:356
  117.3 0.0 copy-start
  117.3 2.4 %copy.13 = f32[128,2048]{1,0:T(8,128)} copy(f32[128,2048]{1,0:T(8,128)} %get-tuple-element.12) | data formatting | bytes 2097152
  119.7 0.0 copy-done
  119.7 0.0 copy-start.1
  119.7 1.0 copy.14
  120.7 0.0 copy-done.1
  120.7 0.6 copy.15
Async XLA Ops:
  0.6 0.7 copy-start.2
  117.3 2.4 %copy-start = (f32[128,2048]{1,0:T(8,128)S(1)}, f32[128,2048]{1,0:T(8,128)}, u32[]{:S(2)}) copy-start(f32[128,2048]{1,0:T(8,128)} %get-tuple-element.13) | copy-start | bytes 3145732
  119.7 1.0 copy-start.1

commit v2 on v1

--- a/solution.py
+++ b/solution.py
@@ -57,8 +57,17 @@
             device_id=(to_i, to_j), device_id_type=MESH,
         )
 
+    inner = a * (3 - a) // 2
+    upper = a // 2
+
+    def plane(s):
+        if far == 1:
+            return a
+        base = (s // 2) * s + (1 - s // 2) * (inner * (1 - s) + (1 - inner) * s)
+        return base + upper * (3 - 2 * base)
+
     def block_of(s, t):
-        return ((a + far - s) % far) * near + (b + near - t) % near
+        return plane(s) * near + (b + near - t) % near
 
     def place(block, quarter):
         return allp.at[aligned(block * n_comp + quarter, piece), :]
@@ -66,8 +75,19 @@
     def own_piece():
         return pts.at[aligned(j, piece), :]
 
-    def z_copy(s):
-        return remote(own_piece(), place(i, j), z_s.at[s], z_r.at[s], ((a + s) % far) * near + b, j)
+    def z_own(d):
+        to = 3 * upper if d else 1 + a % 2
+        return remote(own_piece(), place(i, j), z_s.at[a, d], z_r.at[a], to * near + b, j)
+
+    def z_pass(s, to):
+        src = place(block_of(s, 0), j)
+        return remote(src, src, z_s.at[plane(s), 0], z_r.at[plane(s)], to * near + b, j)
+
+    def z_in(s):
+        return z_pass(s, (a + 1) % far)
+
+    def z_on(s):
+        return z_pass(s, 3 - a if s == 1 else 3 * upper)
 
     def y_copy(s, t):
         src = place(block_of(s, 0), j)
@@ -82,8 +102,13 @@
         src = place(block_of(idx // near, idx % near), quarter)
         return remote(src, src, c_s.at[idx, u], c_r.at[idx, u], i, pair * 2 + 1 - core)
 
-    for s in range(1, far):
-        z_copy(s).start()
+    if far > 1:
+        z_own(0).start()
+
+        @pl.when(inner == 1)
+        def _():
+            z_own(1).start()
+
     allp[aligned(i, rows), :] = pts[...]
     for t in range(1, near):
         y_copy(0, t).start()
@@ -123,15 +148,23 @@
             x_copy(idx, u).start()
         c_copy(idx, 0).start()
 
+    def pass_y(s):
+        for t in range(1, near):
+            y_copy(s, t).wait_recv()
+            pass_on(s * near + t)
+
     for s in range(1, far):
-        z_copy(s).wait_recv()
+        z_in(s).wait_recv()
+
+        @pl.when(inner == 1)
+        def _():
+            z_on(s).start()
+
         for t in range(1, near):
             y_copy(s, t).start()
         pass_on(s * near)
-    for s in range(far):
-        for t in range(1, near):
-            y_copy(s, t).wait_recv()
-            pass_on(s * near + t)
+        pass_y(s - 1)
+    pass_y(far - 1)
 
     def wait_params(r, carry):
         p_copy(r).wait_recv()
@@ -155,12 +188,19 @@
         top = jnp.max(s, 0, keepdims=True)
         part_c[j, pl.ds(block, 1), :] = top + jnp.log(jnp.sum(jnp.exp(s - top), 0, keepdims=True))
 
-    score(i)
-
-    def score_step(idx, carry):
+    def pass_core(idx):
         for u in range(1, pairs):
             x_copy(idx, u).wait_recv()
             c_copy(idx, u).start()
+
+    score(i)
+    pass_core(1)
+
+    def score_step(idx, carry):
+        @pl.when(idx < n_dp - 1)
+        def _():
+            pass_core(idx + 1)
+
         for u in range(pairs):
             c_copy(idx, u).wait_recv()
         score(block_of(idx // near, idx % near))
@@ -316,8 +356,15 @@
         moved = got_m[width : width + 1, :] + got_v[width : width + 1, :]
         out_weight[:, cols] = jnp.where(takes, moved, new_w[:, cols])
 
-    for s in range(1, far):
-        z_copy(s).wait_send()
+    if far > 1:
+        z_own(0).wait_send()
+
+        @pl.when(inner == 1)
+        def _():
+            z_own(1).wait_send()
+            for s in range(1, far):
+                z_on(s).wait_send()
+
     for s in range(far):
         for t in range(1, near):
             y_copy(s, t).wait_send()
@@ -383,7 +430,7 @@
                 pltpu.VMEM((1, k_dev), F32),
                 pltpu.VMEM((2, width + 8, spl), F32),
                 pltpu.VMEM((n_comp, width + 16, 2 * spl), BF),
-                *sem(far), *sem(far, near), *sem(n_dp, pairs), *sem(n_dp, pairs),
+                pltpu.SemaphoreType.DMA((far, 2)), pltpu.SemaphoreType.DMA((far,)), *sem(far, near), *sem(n_dp, pairs), *sem(n_dp, pairs),
                 *sem(n_dp), *sem(n_dp), *sem(n_comp), *sem(n_dp), *sem(n_dp), *sem(n_dp), *sem(n_comp),
             ],
             compiler_params=pltpu.CompilerParams(

time: 121 us -> 117 us (0.967)
  Pallas kernels: 115 us -> 111 us
    pallas_call x1, Pallas kernels: 115 us -> 111 us  [per_device(): pl.pallas_call(functools.partial(kernel, n_dp, n_comp), out_shape=(jax.Sh...]
where the time goes in v2:
time: 117 us
  Pallas kernels  111 us (95%)
  local copies, waits for them, and re-layouts  5.43 us (5%)
    pallas_call x1, Pallas kernels, per_device(): pl.pallas_call(functools.partial(kernel, n_dp, n_comp), out_shape=(jax.Sh...  111 us
    unnamed x10, local copies, waits for them, and re-layouts  5.43 us

profile of v2, /device:TPU:13, one launch (start us, length us, event | category | flops | bytes accessed | tf_op | source)
XLA Modules:
  0.0 116.8 jit_solution(10941443659849043263)
XLA Ops:
  0.6 0.0 copy-start.2
  0.6 0.7 copy-done.2
  1.3 0.8 copy.9.split
  2.1 110.7 %shard_map.85 = (f32[128,2048]{1,0:T(8,128)}, f32[128,2048]{1,0:T(8,128)}, f32[1,2048]{1,0:T(1,128)}) custom-call(bf16[512,1024]{1,0:T(8,128)(2,1)} %pts.1, f32[128,2048]{1,0:T(8,128)} %means.1, f32[128,2048]{1,0:T(8,128)} %variances.1, f32[1,2048]{1,0:T(1,128)} %bitcast.3, s32[256,2]{1,0:T(8,128)} %copy.9.split, s32[1,256]{1,0:T(1,128)} %bitcast.5), custom_call_target="tpu_custom_call" | custom-call | tf_op jit(solution)/shard_map/pallas_call | solution.py:403
  112.8 0.0 copy-start
  112.8 2.4 %copy.13 = f32[128,2048]{1,0:T(8,128)} copy(f32[128,2048]{1,0:T(8,128)} %get-tuple-element.12) | data formatting | bytes 2097152
  115.2 0.0 copy-done
  115.2 0.0 copy-start.1
  115.2 1.0 copy.14
  116.2 0.0 copy-done.1
  116.2 0.6 copy.15
Async XLA Ops:
  0.6 0.7 copy-start.2
  112.8 2.4 %copy-start = (f32[128,2048]{1,0:T(8,128)S(1)}, f32[128,2048]{1,0:T(8,128)}, u32[]{:S(2)}) copy-start(f32[128,2048]{1,0:T(8,128)} %get-tuple-element.13) | copy-start | bytes 3145732
  115.2 1.0 copy-start.1

commit v3 on v2

--- a/solution.py
+++ b/solution.py
@@ -26,8 +26,8 @@
     n_dp, n_comp,
     pts, means, variances, weights, split, prune,
     out_mean, out_var, out_weight,
-    allp, prm, par, par_t, cst_s, cst_r, scores, part_c, part_d, lse, resp,
-    mom_s, mom_r, cnt_s, cnt_r, new_m, new_v, new_w, pay, got,
+    allp, prm, par, par_t, cst_s, cst_r, scores, tops, part_c, part_d, lse, resp,
+    mom_s, mom_r, cnt_s, cnt_r, new_m, new_v, new_w, pay, got, hots,
     z_s, z_r, y_s, y_r, x_s, x_r, c_s, c_r, p_s, p_r, k_s, k_r,
     lc_s, lc_r, ld_s, ld_r, m_s, m_r, n_s, n_r, g_s, g_r,
 ):
@@ -184,9 +184,11 @@
             + lax.dot_general(par_t[1], x, NT, preferred_element_type=F32)
             + const
         )
-        scores[block] = s
         top = jnp.max(s, 0, keepdims=True)
-        part_c[j, pl.ds(block, 1), :] = top + jnp.log(jnp.sum(jnp.exp(s - top), 0, keepdims=True))
+        e = jnp.exp(s - top)
+        scores[block] = e
+        tops[pl.ds(block, 1), :] = top
+        part_c[j, pl.ds(block, 1), :] = top + jnp.log(jnp.sum(e, 0, keepdims=True))
 
     def pass_core(idx):
         for u in range(1, pairs):
@@ -227,10 +229,10 @@
         ld_copy(r).start()
     for r in range(1, n_dp):
         ld_copy(r).wait_recv()
-    lse[...] = joined(part_d[...])
+    lse[...] = jnp.exp(tops[...] - joined(part_d[...]))
 
     def respond(block, carry):
-        value = jnp.exp(scores[block] - lse[pl.ds(block, 1), :]).astype(BF)
+        value = (scores[block] * lse[pl.ds(block, 1), :]).astype(BF)
         resp[:, aligned(block, rows)] = value
         return carry + lax.dot_general(jnp.ones((8, rows), BF), value, NT, preferred_element_type=F32)
 
@@ -302,12 +304,19 @@
         low_high = low.astype(BF)
         low_rest = (low - low_high.astype(F32)).astype(BF)
         here_b = here_f.astype(BF)
-        pay[0, :width, :] += lax.dot_general((mean - shift).astype(BF), here_b, NT, preferred_element_type=F32)
-        pay[1, :width, :] += lax.dot_general(var.astype(BF), here_b, NT, preferred_element_type=F32)
-        spread = lambda row: jnp.broadcast_to(row, (8, chunk))
-        pay[0, width:, :] += lax.dot_general(spread(low_high), here_b, NT, preferred_element_type=F32)
-        pay[1, width:, :] += lax.dot_general(spread(low_rest), here_b, NT, preferred_element_type=F32)
-
+        spread = lambda row: jnp.broadcast_to(row.astype(F32), (8, chunk))
+        stack = jnp.concatenate([mean - shift, var, spread(low_high), spread(low_rest)], 0).astype(BF)
+        pay[...] += lax.dot_general(stack, here_b, NT, preferred_element_type=F32)
+
+    slots = split[:, 1:2]
+    slot_at = lax.broadcasted_iota(jnp.int32, (split.shape[0], split.shape[0]), 1)
+    targets = jnp.sum(jnp.where(slots == slot_at, prune[...].astype(F32), 0.0), 1, keepdims=True) - base
+
+    def mark(at, carry):
+        hots[:, aligned(at, chunk)] = jnp.where(hot(targets, at), 1.0, 0.0).astype(BF)
+        return carry
+
+    lax.fori_loop(0, n_dp, mark, 0)
     finish(i)
 
     def finish_step(r, carry):
@@ -319,10 +328,11 @@
     lax.fori_loop(1, n_dp, finish_step, 0)
 
     extra = 16
-    got[j, :width, :] = jnp.concatenate([pay[0, :width, :], pay[1, :width, :]], 1).astype(BF)
+    ends = 2 * width
+    got[j, :width, :] = jnp.concatenate([pay[:width, :], pay[width:ends, :]], 1).astype(BF)
     got[j, width : width + extra, :] = jnp.concatenate(
         [
-            jnp.concatenate([pay[0, width:, :], pay[1, width:, :]], 1),
+            jnp.concatenate([pay[ends : ends + 8, :], pay[ends + 8 :, :]], 1),
             jnp.ones((8, 2 * spl), F32),
         ],
         0,
@@ -333,28 +343,26 @@
 
     for r in range(1, n_comp):
         g_copy(r).start()
-    slots = split[:, 1:2]
-    slot_at = lax.broadcasted_iota(jnp.int32, (split.shape[0], split.shape[0]), 1)
-    targets = jnp.sum(jnp.where(slots == slot_at, prune[...].astype(F32), 0.0), 1, keepdims=True) - base
-    blank = jnp.full((spl, 1), -1.0, F32)
-    parts = [targets[q * spl : (q + 1) * spl] for q in range(n_comp)]
-    left = jnp.concatenate([part for q in range(n_comp) for part in (parts[q], blank)], 0)
-    right = jnp.concatenate([part for q in range(n_comp) for part in (blank, parts[q])], 0)
     for r in range(1, n_comp):
         g_copy(r).wait_recv()
-    cat = jnp.concatenate([got[q] for q in range(n_comp)], 1)
+    whole = [got[q].astype(F32) for q in range(n_comp)]
+    cat = jnp.concatenate(
+        [
+            jnp.concatenate([part[:, :spl] for part in whole], 1),
+            jnp.concatenate([part[:, spl:] for part in whole], 1),
+        ],
+        0,
+    ).astype(BF)
+    half = width + extra
 
     for at in range(n_dp):
         cols = pl.ds(at * chunk, chunk)
-        hot_l = jnp.where(hot(left, at), 1.0, 0.0).astype(BF)
-        hot_r = jnp.where(hot(right, at), 1.0, 0.0).astype(BF)
-        got_m = jnp.dot(cat, hot_l, preferred_element_type=F32)
-        got_v = jnp.dot(cat, hot_r, preferred_element_type=F32)
-        takes = got_m[width + 8 : width + 9, :] > 0.5
-        out_mean[:, cols] = jnp.where(takes, got_m[:width], new_m[:, cols])
-        out_var[:, cols] = jnp.where(takes, got_v[:width], new_v[:, cols])
-        moved = got_m[width : width + 1, :] + got_v[width : width + 1, :]
-        out_weight[:, cols] = jnp.where(takes, moved, new_w[:, cols])
+        moved = jnp.dot(cat, hots[:, cols], preferred_element_type=F32)
+        takes = moved[width + 8 : width + 9, :] > 0.5
+        out_mean[:, cols] = jnp.where(takes, moved[:width], new_m[:, cols])
+        out_var[:, cols] = jnp.where(takes, moved[half : half + width], new_v[:, cols])
+        weight = moved[width : width + 1, :] + moved[half + width : half + width + 1, :]
+        out_weight[:, cols] = jnp.where(takes, weight, new_w[:, cols])
 
     if far > 1:
         z_own(0).wait_send()
@@ -417,6 +425,7 @@
                 pltpu.VMEM((8, k_dev), F32),
                 pltpu.VMEM((n_dp, 8, chunk), F32),
                 pltpu.VMEM((n_dp, chunk, rows), F32),
+                pltpu.VMEM((n_dp, rows), F32),
                 pltpu.VMEM((n_comp, n_dp, rows), F32),
                 pltpu.VMEM((n_dp, n_dp, rows), F32),
                 pltpu.VMEM((n_dp, rows), F32),
@@ -428,8 +437,9 @@
                 pltpu.VMEM((width, k_dev), F32),
                 pltpu.VMEM((width, k_dev), F32),
                 pltpu.VMEM((1, k_dev), F32),
-                pltpu.VMEM((2, width + 8, spl), F32),
+                pltpu.VMEM((2 * width + 16, spl), F32),
                 pltpu.VMEM((n_comp, width + 16, 2 * spl), BF),
+                pltpu.VMEM((split_list.shape[0], k_dev), BF),
                 pltpu.SemaphoreType.DMA((far, 2)), pltpu.SemaphoreType.DMA((far,)), *sem(far, near), *sem(n_dp, pairs), *sem(n_dp, pairs),
                 *sem(n_dp), *sem(n_dp), *sem(n_comp), *sem(n_dp), *sem(n_dp), *sem(n_dp), *sem(n_comp),
             ],

time: 117 us -> 116 us (level)
  no operation moved by 1% of the time
where the time goes in v3:
time: 116 us
  Pallas kernels  110 us (95%)
  local copies, waits for them, and re-layouts  5.43 us (5%)
    pallas_call x1, Pallas kernels, per_device(): pl.pallas_call(functools.partial(kernel, n_dp, n_comp), out_shape=(jax.Sh...  110 us
    unnamed x10, local copies, waits for them, and re-layouts  5.43 us

profile of v3, /device:TPU:13, one launch (start us, length us, event | category | flops | bytes accessed | tf_op | source)
XLA Modules:
  0.0 116.3 jit_solution(14199778569319469758)
XLA Ops:
  0.6 0.0 copy-start.2
  0.6 0.7 copy-done.2
  1.3 0.8 copy.9.split
  2.1 110.2 %shard_map.85 = (f32[128,2048]{1,0:T(8,128)}, f32[128,2048]{1,0:T(8,128)}, f32[1,2048]{1,0:T(1,128)}) custom-call(bf16[512,1024]{1,0:T(8,128)(2,1)} %pts.1, f32[128,2048]{1,0:T(8,128)} %means.1, f32[128,2048]{1,0:T(8,128)} %variances.1, f32[1,2048]{1,0:T(1,128)} %bitcast.3, s32[256,2]{1,0:T(8,128)} %copy.9.split, s32[1,256]{1,0:T(1,128)} %bitcast.5), custom_call_target="tpu_custom_call" | custom-call | tf_op jit(solution)/shard_map/pallas_call | solution.py:411
  112.3 0.0 copy-start
  112.3 2.4 %copy.13 = f32[128,2048]{1,0:T(8,128)} copy(f32[128,2048]{1,0:T(8,128)} %get-tuple-element.12) | data formatting | bytes 2097152
  114.7 0.0 copy-done
  114.7 0.0 copy-start.1
  114.7 1.0 copy.14
  115.7 0.0 copy-done.1
  115.7 0.6 copy.15
Async XLA Ops:
  0.6 0.7 copy-start.2
  112.3 2.4 %copy-start = (f32[128,2048]{1,0:T(8,128)S(1)}, f32[128,2048]{1,0:T(8,128)}, u32[]{:S(2)}) copy-start(f32[128,2048]{1,0:T(8,128)} %get-tuple-element.13) | copy-start | bytes 3145732
  114.7 1.0 copy-start.1

commit v4 on v3

--- a/solution.py
+++ b/solution.py
@@ -132,14 +132,16 @@
         to = (i + r) % n_dp
         return remote(cst_s.at[:, aligned(to, chunk)], cst_r.at[i], k_s.at[r], k_r.at[r], to, j)
 
+    def each_params(r, carry):
+        make_params((i + r) % n_dp)
+        return carry
+
     def send_params(r, carry):
-        make_params((i + r) % n_dp)
         p_copy(r).start()
         k_copy(r).start()
         return carry
 
-    lax.fori_loop(1, n_dp, send_params, 0)
-    make_params(i)
+    lax.fori_loop(0, n_dp, each_params, 0)
     par[:, aligned(i, width), :] = prm[:, :, aligned(i, chunk)]
     cst_r[i] = cst_s[:, aligned(i, chunk)]
 
@@ -164,7 +166,11 @@
             y_copy(s, t).start()
         pass_on(s * near)
         pass_y(s - 1)
+        if s == 1:
+            lax.fori_loop(1, n_dp, send_params, 0)
     pass_y(far - 1)
+    if far == 1:
+        lax.fori_loop(1, n_dp, send_params, 0)
 
     def wait_params(r, carry):
         p_copy(r).wait_recv()

time: 116 us -> 117 us (level)
  no operation moved by 1% of the time
where the time goes in v4:
time: 117 us
  Pallas kernels  111 us (95%)
  local copies, waits for them, and re-layouts  5.43 us (5%)
    pallas_call x1, Pallas kernels, per_device(): pl.pallas_call(functools.partial(kernel, n_dp, n_comp), out_shape=(jax.Sh...  111 us
    unnamed x10, local copies, waits for them, and re-layouts  5.43 us

profile of v4, /device:TPU:13, one launch (start us, length us, event | category | flops | bytes accessed | tf_op | source)
XLA Modules:
  0.0 116.9 jit_solution(3870016129623849766)
XLA Ops:
  0.6 0.0 copy-start.2
  0.6 0.7 copy-done.2
  1.3 0.8 copy.9.split
  2.1 110.8 %shard_map.85 = (f32[128,2048]{1,0:T(8,128)}, f32[128,2048]{1,0:T(8,128)}, f32[1,2048]{1,0:T(1,128)}) custom-call(bf16[512,1024]{1,0:T(8,128)(2,1)} %pts.1, f32[128,2048]{1,0:T(8,128)} %means.1, f32[128,2048]{1,0:T(8,128)} %variances.1, f32[1,2048]{1,0:T(1,128)} %bitcast.3, s32[256,2]{1,0:T(8,128)} %copy.9.split, s32[1,256]{1,0:T(1,128)} %bitcast.5), custom_call_target="tpu_custom_call" | custom-call | tf_op jit(solution)/shard_map/pallas_call | solution.py:417
  113.0 0.0 copy-start
  113.0 2.4 %copy.13 = f32[128,2048]{1,0:T(8,128)} copy(f32[128,2048]{1,0:T(8,128)} %get-tuple-element.12) | data formatting | bytes 2097152
  115.4 0.0 copy-done
  115.4 0.0 copy-start.1
  115.4 1.0 copy.14
  116.3 0.0 copy-done.1
  116.3 0.6 copy.15
Async XLA Ops:
  0.6 0.7 copy-start.2
  113.0 2.4 %copy-start = (f32[128,2048]{1,0:T(8,128)S(1)}, f32[128,2048]{1,0:T(8,128)}, u32[]{:S(2)}) copy-start(f32[128,2048]{1,0:T(8,128)} %get-tuple-element.13) | copy-start | bytes 3145732
  115.4 1.0 copy-start.1

commit v5 on v4

--- a/solution.py
+++ b/solution.py
@@ -97,6 +97,10 @@
         src = place(block_of(idx // near, idx % near), j)
         return remote(src, src, x_s.at[idx, u], x_r.at[idx, u], i, ((pair + u) % pairs) * 2 + core)
 
+    def yx_copy(t, u):
+        src = place(i, ((pair + pairs - u) % pairs) * 2 + core)
+        return remote(src, src, x_s.at[t, u], x_r.at[t, u], a * near + (b + t) % near, j)
+
     def c_copy(idx, u):
         quarter = ((pair + pairs - u) % pairs) * 2 + core
         src = place(block_of(idx // near, idx % near), quarter)
@@ -112,6 +116,8 @@
     allp[aligned(i, rows), :] = pts[...]
     for t in range(1, near):
         y_copy(0, t).start()
+        for u in range(1, pairs):
+            yx_copy(t, u).start()
 
     def make_params(to):
         cols = aligned(to, chunk)
@@ -146,8 +152,9 @@
     cst_r[i] = cst_s[:, aligned(i, chunk)]
 
     def pass_on(idx):
-        for u in range(1, pairs):
-            x_copy(idx, u).start()
+        if idx >= near:
+            for u in range(1, pairs):
+                x_copy(idx, u).start()
         c_copy(idx, 0).start()
 
     def pass_y(s):

time: 117 us -> 117 us (level)
  no operation moved by 1% of the time
where the time goes in v5:
time: 117 us
  Pallas kernels  111 us (95%)
  local copies, waits for them, and re-layouts  5.43 us (5%)
    pallas_call x1, Pallas kernels, per_device(): pl.pallas_call(functools.partial(kernel, n_dp, n_comp), out_shape=(jax.Sh...  111 us
    unnamed x10, local copies, waits for them, and re-layouts  5.43 us

profile of v5, /device:TPU:13, one launch (start us, length us, event | category | flops | bytes accessed | tf_op | source)
XLA Modules:
  0.0 116.8 jit_solution(16273853267597262114)
XLA Ops:
  0.6 0.0 copy-start.2
  0.6 0.7 copy-done.2
  1.3 0.8 copy.9.split
  2.1 110.7 %shard_map.85 = (f32[128,2048]{1,0:T(8,128)}, f32[128,2048]{1,0:T(8,128)}, f32[1,2048]{1,0:T(1,128)}) custom-call(bf16[512,1024]{1,0:T(8,128)(2,1)} %pts.1, f32[128,2048]{1,0:T(8,128)} %means.1, f32[128,2048]{1,0:T(8,128)} %variances.1, f32[1,2048]{1,0:T(1,128)} %bitcast.3, s32[256,2]{1,0:T(8,128)} %copy.9.split, s32[1,256]{1,0:T(1,128)} %bitcast.5), custom_call_target="tpu_custom_call" | custom-call | tf_op jit(solution)/shard_map/pallas_call | solution.py:424
  112.9 0.0 copy-start
  112.9 2.4 %copy.13 = f32[128,2048]{1,0:T(8,128)} copy(f32[128,2048]{1,0:T(8,128)} %get-tuple-element.12) | data formatting | bytes 2097152
  115.2 0.0 copy-done
  115.2 0.0 copy-start.1
  115.3 1.0 copy.14
  116.2 0.0 copy-done.1
  116.2 0.6 copy.15
Async XLA Ops:
  0.6 0.7 copy-start.2
  112.9 2.4 %copy-start = (f32[128,2048]{1,0:T(8,128)S(1)}, f32[128,2048]{1,0:T(8,128)}, u32[]{:S(2)}) copy-start(f32[128,2048]{1,0:T(8,128)} %get-tuple-element.13) | copy-start | bytes 3145732
  115.2 1.0 copy-start.1
